TPU v7x, 32 devices: a whole 2x2x4 slice. The times are simulated.
32 devices in a mesh: tank: 2 (over y), slab: 4 (over z), cross: 2 (over x), sub: 2 (over core).
Axes of the slice: x: 2, y: 2, z: 4, core: 2. Of those that a mesh axis runs over, the one named last changes fastest.
Arguments:
- positions: float32 [3, 64, 64, 128], P(None, ('tank', 'slab'), ('cross', 'sub')), parts along dimension 1, as said below
- velocities: float32 [3, 64, 64, 128], P(None, ('tank', 'slab'), ('cross', 'sub')), parts along dimension 1, may hold values from -6 to 6
- pair_i: int32 [8, 4, 1152], P(('tank', 'slab'), ('cross', 'sub')), parts along dimension 0, may hold values from 0 to 127, as said below
- pair_j: int32 [8, 4, 1152], P(('tank', 'slab'), ('cross', 'sub')), parts along dimension 0, may hold values from 0 to 179, as said below
- pair_count: int32 [8, 4], P(('tank', 'slab'), ('cross', 'sub')), parts along dimension 0, may hold values from 128 to 1152, as said below
- block_fill: int32 [64, 64], P(('tank', 'slab'), ('cross', 'sub')), parts along dimension 0, may hold values from 0 to 128, as said below
- block_body: int32 [64, 64], P(('tank', 'slab'), ('cross', 'sub')), parts along dimension 0, may hold values from 0 to 4
Outputs:
- density: float32 [64, 64, 128], P(('tank', 'slab'), ('cross', 'sub')), parts along dimension 0
- accel: float32 [3, 64, 64, 128], P(None, ('tank', 'slab'), ('cross', 'sub')), parts along dimension 1
- body_force: float32 [3, 8], P(None, 'tank'), parts along dimension 1
There are 2 independent parts, one for each index of `tank`. A program takes and returns all parts, laid end to end along the dimension named above; each array names one. Nothing has to cross between parts.
Inputs may be any that keep to these rules, and one draw needn't show every extreme that they name: `pair_i`: slots 0 to 127 of each row pair local block k with itself (extended block (k // 16 + 1) (18) + k % 16 + 1); the other slots pair each local block once with each of its eight neighbouring extended blocks, in a drawn order, those in which both blocks lie in the tank and have block_fill above 0 coming first. `pair_j`: see pair_i. pair_count is 128 plus the number of neighbour slots whose two blocks both lie in the tank and have block_fill above 0. `block_fill`: a block holds either no particles or 64 to 128. `block_body`: the value 4 marks a free fluid block. `positions`: particles of global block (a, b) have first coordinate in [2.6 a, 2.6 (a + 1)), second in [2.6 b, 2.6 (b + 1)) and third in [0, 18.9).
All inputs are finite; a program needn't handle non-finite values.
Results may differ from a plain program's by a relative error of at most 0.0003.
Values sent between devices are 32-bit elements; how exact they have to be, the bound alone decides.
A program may use at most 64 MiB of HBM per device.

v0:
```python
import math

import jax
import jax.numpy as jnp
from jax import lax
from jax.sharding import PartitionSpec as P

NBODY = 4


SMOOTH = 1.3
KERNEL_NORM = 21.0 / (16.0 * math.pi * SMOOTH**3)
SLOPE_NORM = 5.0 * KERNEL_NORM / SMOOTH**2
VISCOSITY = 0.2
GRAVITY = 1.0


def padded(shard, sides, width):
    for axis, dim in sides:
        devices, length = (lax.axis_size(axis), shard.shape[dim])
        up = [(i, (i + 1) % devices) for i in range(devices - 1)]
        down = [(j, i) for i, j in up]
        last = lax.slice_in_dim(shard, length - width, length, axis=dim)
        initial = lax.slice_in_dim(shard, 0, width, axis=dim)
        before = lax.ppermute(last, axis, up)
        after = lax.ppermute(initial, axis, down)
        shard = jnp.concatenate([before, shard, after], axis=dim)
    return shard


def pair_shape(first_tiles, second_tiles):
    offsets = first_tiles[:, 0:3, :, None] - second_tiles[:, 0:3, None, :]
    distance = jnp.sqrt(jnp.sum(offsets * offsets, axis=1)) / SMOOTH
    remain = jnp.maximum(1.0 - 0.5 * distance, 0.0)
    return (offsets, distance, remain)


def density_terms(first_tiles, second_tiles):
    offsets, distance, remain = pair_shape(first_tiles, second_tiles)
    kernel = KERNEL_NORM * remain**4 * (2.0 * distance + 1.0)
    return jnp.sum(kernel * second_tiles[:, 3, None, :], axis=2)


def force_terms(first_tiles, second_tiles):
    offsets, distance, remain = pair_shape(first_tiles, second_tiles)
    slope = SLOPE_NORM * remain**3 * second_tiles[:, 3, None, :]
    pushed = slope * (first_tiles[:, 7, :, None] + second_tiles[:, 7, None, :])
    push_sum = jnp.sum(pushed[:, None] * offsets, axis=3)
    drift = first_tiles[:, 4:7, :, None] - second_tiles[:, 4:7, None, :]
    drag_sum = jnp.sum(slope[:, None] * drift, axis=3)
    return push_sum - VISCOSITY * drag_sum


def tile_loop(
    begin_slot, end_slot, total_slots, group_size, fetch_tiles, kernel, store_values, initial
):
    first_group = begin_slot // group_size
    last_group = (end_slot + group_size - 1) // group_size

    def advance(group_index, carried):
        nominal = group_index * group_size
        anchor = jnp.minimum(nominal, total_slots - group_size).astype(jnp.int32)
        slot_ids = anchor + lax.broadcasted_iota(jnp.int32, (group_size,), 0)
        wanted = (slot_ids >= jnp.maximum(begin_slot, nominal)) & (
            slot_ids < jnp.minimum(end_slot, nominal + group_size)
        )
        first_tiles, second_tiles = fetch_tiles(anchor)
        values = kernel(first_tiles, second_tiles)
        weight = wanted.astype(jnp.float32).reshape((group_size,) + (1,) * (values.ndim - 1))
        return store_values(carried, anchor, values * weight)

    return lax.fori_loop(first_group, last_group, advance, initial)


def table_fetch(table, firsts, seconds, group_size):

    def fetch_tiles(anchor):
        first_ids = lax.dynamic_slice_in_dim(firsts, anchor, group_size)
        second_ids = lax.dynamic_slice_in_dim(seconds, anchor, group_size)
        return (jnp.take(table, first_ids, axis=0), jnp.take(table, second_ids, axis=0))

    return fetch_tiles


def scatter_store(targets, group_size):

    def store_values(carried, anchor, values):
        target_ids = lax.dynamic_slice_in_dim(targets, anchor, group_size)
        return carried.at[target_ids].add(values)

    return store_values


def shards(positions, velocities, pair_i, pair_j, pair_count, block_fill, block_body):
    lengthwise, columns = block_fill.shape
    local_count = lengthwise * columns
    frame_width = columns + 2
    slot_ids = lax.broadcasted_iota(jnp.int32, (lengthwise, columns, 128), 2)
    masses = (slot_ids < block_fill[:, :, None]).astype(jnp.float32)
    state = jnp.concatenate(
        [
            jnp.transpose(positions, (1, 2, 0, 3)),
            masses[:, :, None, :],
            jnp.transpose(velocities, (1, 2, 0, 3)),
        ],
        axis=2,
    )
    framed = padded(state, (("slab", 0), (("cross", "sub"), 1)), 1)
    table = framed.reshape((lengthwise + 2) * frame_width, 7, 128)
    local_firsts = pair_i.reshape(-1)
    ext_firsts = (local_firsts // columns + 1) * frame_width + local_firsts % columns + 1
    ext_seconds = pair_j.reshape(-1)
    total_slots = local_firsts.shape[0]
    live_count = pair_count.reshape(())
    group_size = min(16, 2 * local_count, total_slots)
    density_sums = tile_loop(
        0,
        live_count,
        total_slots,
        group_size,
        table_fetch(table, ext_firsts, ext_seconds, group_size),
        density_terms,
        scatter_store(local_firsts, group_size),
        jnp.zeros((local_count, 128), jnp.float32),
    )
    valid = masses.reshape(local_count, 128)
    density = density_sums * valid
    safe_density = jnp.where(valid > 0, density_sums, 1.0)
    pressure_term = valid * (safe_density**7 - 1.0) / (safe_density * safe_density)
    framed_pressure = padded(
        pressure_term.reshape(lengthwise, columns, 1, 128), (("slab", 0), (("cross", "sub"), 1)), 1
    )
    force_table = jnp.concatenate([table, framed_pressure.reshape(-1, 1, 128)], axis=1)
    hydro_start = jnp.zeros((local_count, 3, 128), jnp.float32)
    hydro = tile_loop(
        0,
        live_count,
        total_slots,
        group_size,
        table_fetch(force_table, ext_firsts, ext_seconds, group_size),
        force_terms,
        scatter_store(local_firsts, group_size),
        hydro_start,
    )
    hydro = hydro * valid[:, None, :]
    nothing = jnp.zeros_like(valid)
    gravity = jnp.stack([nothing, nothing, GRAVITY * valid], axis=1)
    accel = jnp.transpose((hydro - gravity).reshape(lengthwise, columns, 3, 128), (2, 0, 1, 3))
    block_sums = jnp.sum(hydro, axis=2)
    owners = (
        block_body.reshape(local_count)[:, None]
        == lax.broadcasted_iota(jnp.int32, (local_count, NBODY), 1)
    ).astype(jnp.float32)
    partial_force = jnp.dot(block_sums.T, owners, precision=lax.Precision.HIGHEST)
    totals = lax.psum(partial_force, ("slab", "cross", "sub"))
    slot_total = (
        128
        * lengthwise
        * lax.axis_size("slab")
        * columns
        * lax.axis_size("cross")
        * lax.axis_size("sub")
    )
    body_force = totals / math.sqrt(slot_total)
    return (density.reshape(lengthwise, columns, 128), accel, body_force)


def solution(mesh):
    placed = (
        P(None, ("tank", "slab"), ("cross", "sub"), None),
        P(None, ("tank", "slab"), ("cross", "sub"), None),
        P(("tank", "slab"), ("cross", "sub"), None),
        P(("tank", "slab"), ("cross", "sub"), None),
        P(("tank", "slab"), ("cross", "sub")),
        P(("tank", "slab"), ("cross", "sub")),
        P(("tank", "slab"), ("cross", "sub")),
    )
    return jax.shard_map(
        shards,
        mesh=mesh,
        in_specs=placed,
        out_specs=(
            P(("tank", "slab"), ("cross", "sub"), None),
            P(None, ("tank", "slab"), ("cross", "sub"), None),
            P(None, "tank"),
        ),
        check_vma=False,
    )
```

profile of v0, /device:TPU:0, one launch (start us, length us, event | category | flops | bytes accessed | tf_op | source)
XLA Modules:
  0.0 1040.7 jit_solution(2760082690979434666)
XLA Ops:
  2.3 4.9 collective-permute-start
  7.3 1.3 collective-permute-start.1
  9.3 4.1 collective-permute-done.1
  17.8 2.7 collective-permute-done.3
  21.0 124.1 %while.24 = (s32[]{:T(128)}, f32[128,128]{1,0:T(8,128)S(1)}, s32[]{:T(128)}, s32[1152]{0:T(1024)S(1)}, s32[1152]{0:T(1024)S(1)}, /*index=5*/f32[180,7,128]{2,1,0...) while((s32[]{:T(128)}, f32[128,128]{1,0:T(8,128)S(1)}, ...), condition=%wide.region_4.6_spmd, body=%wide.region_0.5_spmd.sunk | while | flops 5005642 | bytes 2704879 | solution.py:72
  145.8 27.3 %collective-permute-start.4 = (f32[1,16,1,128]{3,1,2,0:T(8,128)S(1)}, f32[1,16,1,128]{3,1,2,0:T(8,128)S(1)}, u32[]{:S(2)}, u32[]{:S(2)}) collective-permute-start(f32[1,16,1,128]{3,1,2,0:T(8,128)S(1)} %get-tuple-element.278), channel_id=1, source_target_pairs={{0,4},{4,8},{8,12},{1,5},{5,9},{9,13},{2,6},{6,10},{10,14},{3,7},{... | collective-permute-start | bytes 24584 | tf_op jit(solution)/shard_map/ppermute | solution.py:25
  173.1 1.3 collective-permute-start.5
  174.5 194.6 %collective-permute-done.5 = f32[1,16,1,128]{3,1,2,0:T(8,128)S(1)} collective-permute-done((f32[1,16,1,128]{3,1,2,0:T(8,128)S(1)}, f32[1,16,1,128]{3,1,2,0:T(8,128)S(1)}, u32[]{:S(2)}, u32[]{:S(2)}) %collective-permute-start.5) | collective-permute-done | bytes 8224 | tf_op jit(solution)/shard_map/ppermute | solution.py:26
  369.1 8.2 collective-permute-start.6
  378.9 2.1 collective-permute-done.7
  381.3 229.4 %while.25 = (s32[]{:T(128)}, f32[128,3,128]{2,1,0:T(4,128)S(1)}, s32[]{:T(128)}, s32[1152]{0:T(1024)S(1)}, s32[1152]{0:T(1024)S(1)}, /*index=5*/f32[180,8,128]{2...) while((s32[]{:T(128)}, f32[128,3,128]{2,1,0:T(4,128)S(1)}, ...), condition=%wide.region_10.13_spmd, body=%wide.region_5.12_spmd.sunk | while | flops 8962378 | bytes 7439471 | solution.py:72
  384.4 1.9 multiply_reduce_fusion.9
  386.3 1.9 fusion.35
  393.2 1.9 multiply_reduce_fusion.9
  395.1 1.9 fusion.35
  402.1 1.9 multiply_reduce_fusion.9
  403.9 1.9 fusion.35
  410.9 1.9 multiply_reduce_fusion.9
  412.8 1.9 fusion.35
  419.7 1.9 multiply_reduce_fusion.9
  421.6 1.9 fusion.35
  428.5 1.9 multiply_reduce_fusion.9
  430.4 1.9 fusion.35
  437.4 1.9 multiply_reduce_fusion.9
  439.2 1.9 fusion.35
  446.2 1.9 multiply_reduce_fusion.9
  448.0 1.9 fusion.35
  455.0 1.9 multiply_reduce_fusion.9
  456.9 1.9 fusion.35
  463.8 1.9 multiply_reduce_fusion.9
  465.7 1.9 fusion.35
  472.6 1.9 multiply_reduce_fusion.9
  474.5 1.9 fusion.35
  481.5 1.9 multiply_reduce_fusion.9
  483.3 1.9 fusion.35
  490.3 1.9 multiply_reduce_fusion.9
  492.2 1.9 fusion.35
  499.1 1.9 multiply_reduce_fusion.9
  501.0 1.9 fusion.35
  507.9 1.9 multiply_reduce_fusion.9
  509.8 1.9 fusion.35
  516.8 1.9 multiply_reduce_fusion.9
  518.6 1.9 fusion.35
  525.6 1.9 multiply_reduce_fusion.9
  527.5 1.9 fusion.35
  534.4 1.9 multiply_reduce_fusion.9
  536.3 1.9 fusion.35
  543.2 1.9 multiply_reduce_fusion.9
  545.1 1.9 fusion.35
  552.1 1.9 multiply_reduce_fusion.9
  553.9 1.9 fusion.35
  560.9 1.9 multiply_reduce_fusion.9
  562.8 1.9 fusion.35
  569.7 1.9 multiply_reduce_fusion.9
  571.6 1.9 fusion.35
  578.5 1.9 multiply_reduce_fusion.9
  580.4 1.9 fusion.35
  587.4 1.9 multiply_reduce_fusion.9
  589.2 1.9 fusion.35
  596.2 1.9 multiply_reduce_fusion.9
  598.1 1.9 fusion.35
  605.0 1.9 multiply_reduce_fusion.9
  606.9 1.9 fusion.35
  611.9 428.2 %psum.7 = f32[3,4]{1,0:T(4,128)S(1)} all-reduce(f32[3,4]{1,0:T(4,128)S(1)} %fusion.12), channel_id=1, replica_groups=mesh['tank'=2,'slab'=4,'cross'=2,'sub'=2] {'slab','cross','sub'}, use_global_device_ids=true, to_apply=%region_12.15 | all-reduce | flops 12 | bytes 96 | tf_op jit(solution)/shard_map/psum | solution.py:155
  (846 shorter events, 226.7 us)
Async XLA Ops:
  0.6 17.1 %copy-start.2 = (s32[8,16]{1,0:T(8,128)S(1)}, s32[8,16]{1,0:T(8,128)}, u32[]{:S(2)}) copy-start(s32[8,16]{1,0:T(8,128)} %param.20) | copy-start | bytes 1540
  0.6 19.9 %copy-start.1 = (f32[3,8,16,128]{3,2,1,0:T(8,128)S(1)}, f32[3,8,16,128]{3,2,1,0:T(8,128)}, u32[]{:S(2)}) copy-start(f32[3,8,16,128]{3,2,1,0:T(8,128)} %param.15) | copy-start | bytes 589828
  0.7 19.9 %copy-start = (f32[3,8,16,128]{3,2,1,0:T(8,128)S(1)}, f32[3,8,16,128]{3,2,1,0:T(8,128)}, u32[]{:S(2)}) copy-start(f32[3,8,16,128]{3,2,1,0:T(8,128)} %param.16) | copy-start | bytes 589828
  0.7 17.1 %copy-start.3 = (s32[1,1,1152]{2,1,0:T(1,128)S(1)}, s32[1,1,1152]{2,1,0:T(1,128)}, u32[]{:S(2)}) copy-start(s32[1,1,1152]{2,1,0:T(1,128)} %param.18) | copy-start | bytes 13828
  2.3 7.0 collective-permute-start
  7.3 6.1 collective-permute-start.1
  14.4 3.4 collective-permute-start.2
  15.7 4.8 collective-permute-start.3
  21.0 357.8 %copy-start.4 = (s32[8,16]{1,0:T(8,128)S(1)}, s32[8,16]{1,0:T(8,128)}, u32[]{:S(2)}) copy-start(s32[8,16]{1,0:T(8,128)} %param.21) | copy-start | bytes 1540
  145.8 28.7 %collective-permute-start.4 = (f32[1,16,1,128]{3,1,2,0:T(8,128)S(1)}, f32[1,16,1,128]{3,1,2,0:T(8,128)S(1)}, u32[]{:S(2)}, u32[]{:S(2)}) collective-permute-start(f32[1,16,1,128]{3,1,2,0:T(8,128)S(1)} %get-tuple-element.278), channel_id=1, source_target_pairs={{0,4},{4,8},{8,12},{1,5},{5,9},{9,13},{2,6},{6,10},{10,14},{3,7},{... | collective-permute-start | bytes 24584 | tf_op jit(solution)/shard_map/ppermute | solution.py:25
  173.1 196.0 %collective-permute-start.5 = (f32[1,16,1,128]{3,1,2,0:T(8,128)S(1)}, f32[1,16,1,128]{3,1,2,0:T(8,128)S(1)}, u32[]{:S(2)}, u32[]{:S(2)}) collective-permute-start(f32[1,16,1,128]{3,1,2,0:T(8,128)S(1)} %get-tuple-element.279), channel_id=1, source_target_pairs={{4,0},{8,4},{12,8},{5,1},{9,5},{13,9},{6,2},{10,6},{14,10},{7,3},{... | collective-permute-start | bytes 24584 | tf_op jit(solution)/shard_map/ppermute | solution.py:26
  369.1 9.8 collective-permute-start.6
  377.3 3.7 collective-permute-start.7
where the time goes:
time: 1040 us
  blocking collectives  428 us (41%)
  other arithmetic  258 us (25%)
  waiting for transfers between devices  203 us (20%)
  local copies, waits for them, and re-layouts  61.4 us (6%)
  starting transfers between devices  46.9 us (5%)
  loops' own time  40.8 us (4%)
    psum x1, blocking collectives, shards(): totals = lax.psum(partial_force, ('slab', 'cross', 'sub'))  428 us
    ppermute x4, waiting for transfers between devices, padded(): after = lax.ppermute(initial, axis, down)  203 us
    reduce_sum x52, other arithmetic, pair_shape(): distance = jnp.sqrt(jnp.sum(offsets * offsets, axis=1)) / SMOOTH  54 us
    reduce_sum x26, other arithmetic, force_terms(): drag_sum = jnp.sum(slope[:, None] * drift, axis=3)  48.5 us
    reduce_sum x26, other arithmetic, force_terms(): push_sum = jnp.sum(pushed[:, None] * offsets, axis=3)  48.5 us
    scatter-add x52, other arithmetic, store_values(): return carried.at[target_ids].add(values)  48.4 us
    ppermute x4, starting transfers between devices, padded(): before = lax.ppermute(last, axis, up)  41.7 us
    another operation x2, loops' own time, tile_loop(): return lax.fori_loop(first_group, last_group, advance, initial)  40.8 us
  transfers between devices with their start and end apart: 8, of which 4 were waited for; matrix products, arithmetic and copies ran while one was open for 0% of the time, Pallas kernels for 0%

commit v1 on v0

v1 whole, which is shorter than its diff:
```python
import math

import jax
import jax.numpy as jnp
import numpy as np
from jax import lax
from jax.experimental import pallas as pl
from jax.experimental.pallas import tpu as pltpu
from jax.sharding import PartitionSpec as P

NBODY = 4
SMOOTH = 1.3
CELL = 2.6
KERNEL_NORM = 21.0 / (16.0 * math.pi * SMOOTH**3)
SLOPE_NORM = 5.0 * KERNEL_NORM / SMOOTH**2
VISCOSITY = 0.2
GRAVITY = 1.0
FAR = 64.0
TINY = 1e-12
STEPS = [(da, db) for da in (-1, 0, 1) for db in (-1, 0, 1)]
FEAT = 64
F32, BF16 = jnp.float32, jnp.bfloat16


def shift_tables():
    scale = np.zeros((9, 8, 8, 128), np.float32)
    added = np.zeros((9, 8, 8, 128), np.float32)
    for k, (da, db) in enumerate(STEPS):
        scale[k, 0:6, 0:4] = 1.0
        scale[k, 0:3, 4] = 1.0
        scale[k, 0:3, 7] = -2.0 * da
        scale[k, 6, 4] = scale[k, 6, 7] = scale[k, 7, 4] = -2.0 * db
        for g in (0, 3, 5):
            added[k, g, 5] = 2.0 * da
            added[k, g, 6] = 2.0 * db
        added[k, 7, 7] = da * da + db * db
    return (
        jnp.asarray(scale.reshape(9, FEAT, 128), BF16),
        jnp.asarray(added.reshape(9, FEAT, 128), BF16),
    )


def split3(value):
    high = value.astype(BF16).astype(F32)
    rest = value - high
    middle = rest.astype(BF16).astype(F32)
    return high, middle, rest - middle


def norm_row(block):
    square = block * block
    return square[0:1] + square[1:2] + square[2:3]


def second_features(block):
    mass = block[3:4]
    x, y, z = block[0:1] * mass, block[1:2] * mass, block[2:3] * mass
    norm = jnp.where(mass > 0, norm_row(block), FAR)
    one = jnp.ones_like(mass)
    high, middle, low = split3(jnp.concatenate([x, y, z, norm, one, x, y, one], axis=0))
    rows = jnp.concatenate([high, high, high, middle, middle, low, high, high], axis=0)
    return rows.T.astype(BF16)


def first_features(block):
    x, y, z = block[0:1], block[1:2], block[2:3]
    zero = jnp.zeros_like(x)
    norm = norm_row(block)
    high, middle, low = split3(
        jnp.concatenate([-2.0 * x, -2.0 * y, -2.0 * z, zero, norm, y, zero, x], axis=0)
    )
    row = lax.broadcasted_iota(jnp.int32, (8, 128), 0)
    unit = (row == 3).astype(F32)
    g0, g1, g2 = high + unit, middle, low
    g6 = jnp.concatenate(
        [zero, zero, zero, zero, high[5:6], zero, zero, middle[5:6]], axis=0
    )
    g7 = jnp.concatenate([zero, zero, zero, zero, low[5:6], zero, zero, zero], axis=0)
    return jnp.concatenate([g0, g1, g2, g0, g1, g0, g6, g7], axis=0).astype(BF16)


def closeness(second, base, scale, added):
    first = base * scale + added
    square = jnp.dot(second, first, preferred_element_type=F32)
    square = jnp.maximum(square, TINY)
    return jnp.maximum(1.0 - square * lax.rsqrt(square), 0.0)


def density_kernel(length, width, e_ref, scale_ref, added_ref, a_ref, dens_ref, press_ref):
    frame = width + 2

    def prepare(e, carry):
        a_ref[e] = second_features(e_ref[e])
        return carry

    lax.fori_loop(0, (length + 2) * frame, prepare, 0)

    def local(i, carry):
        row, column = i // width, i % width
        centre = (row + 1) * frame + column + 1
        block = e_ref[centre]
        base = first_features(block)
        total = jnp.zeros((8, 128), F32)
        for k, (da, db) in enumerate(STEPS):
            rest = closeness(
                a_ref[centre + da * frame + db], base, scale_ref[k], added_ref[k]
            )
            twice = rest * rest
            value = twice * twice * (1.25 - rest)
            total = total + jnp.sum(value.reshape(16, 8, 128), axis=0)
        mass = block[3:4]
        raw = (4.0 * KERNEL_NORM) * jnp.sum(total, axis=0, keepdims=True)
        dens_ref[row, pl.ds(column, 1), :] = raw * mass
        safe = jnp.where(mass > 0, raw, 1.0)
        square = safe * safe
        seventh = square * square * square * safe
        press_ref[row, pl.ds(column, 1), :] = mass * (seventh - 1.0) / square
        return carry

    lax.fori_loop(0, length * width, local, 0)


def force_kernel(
    length, width, e_ref, a_ref, p_ref, scale_ref, added_ref, hydro_ref, c_ref
):
    frame = width + 2

    def placed(block, row, column):
        lane = lax.broadcasted_iota(jnp.int32, (1, 128), 1)
        along = jnp.zeros_like(lane) + (row - length // 2)
        across = jnp.zeros_like(lane) + (column - width // 2)
        return (
            block[0:1] + along.astype(F32),
            block[1:2] + across.astype(F32),
            block[2:3],
        )

    def prepare(e, carry):
        row, column = e // frame, e % frame
        block = e_ref[e]
        mass = block[3:4]
        pressure = p_ref[row, pl.ds(column, 1), :]
        spots = placed(block, row - 1, column - 1)
        rows = [mass, pressure] + [spot * mass for spot in spots]
        for d in range(3):
            rows.append(
                mass * (VISCOSITY * block[4 + d : 5 + d] - CELL * pressure * spots[d])
            )
        high, middle, low = split3(jnp.concatenate(rows, axis=0))
        part = jnp.concatenate(
            [high, middle, low, jnp.zeros_like(low)], axis=0
        ).astype(BF16)
        c_ref[e] = jnp.concatenate([part, part], axis=1)
        return carry

    lax.fori_loop(0, (length + 2) * frame, prepare, 0)

    def local(i, carry):
        row, column = i // width, i % width
        centre = (row + 1) * frame + column + 1
        block = e_ref[centre]
        base = first_features(block)
        total = jnp.zeros((32, 128), F32)
        for k, (da, db) in enumerate(STEPS):
            e = centre + da * frame + db
            rest = closeness(a_ref[e], base, scale_ref[k], added_ref[k])
            slope = rest * rest * rest
            high = slope.astype(BF16)
            low = (slope - high.astype(F32)).astype(BF16)
            total = total + jnp.dot(
                c_ref[e],
                jnp.concatenate([high, low], axis=0),
                preferred_element_type=F32,
            )
        sums = total[0:8] + total[8:16] + total[16:24]
        mass = block[3:4]
        pressure = p_ref[row + 1, pl.ds(column + 1, 1), :]
        spots = placed(block, row, column)
        for d in range(3):
            own = CELL * pressure * spots[d] - VISCOSITY * block[4 + d : 5 + d]
            value = (
                own * sums[0:1]
                + CELL * (spots[d] * sums[1:2] - pressure * sums[2 + d : 3 + d])
                + sums[5 + d : 6 + d]
            )
            hydro_ref[d, row, pl.ds(column, 1), :] = SLOPE_NORM * mass * value
        return carry

    lax.fori_loop(0, length * width, local, 0)


def padded(shard, sides, width):
    for axis, dim in sides:
        devices, length = (lax.axis_size(axis), shard.shape[dim])
        up = [(i, (i + 1) % devices) for i in range(devices - 1)]
        down = [(j, i) for i, j in up]
        last = lax.slice_in_dim(shard, length - width, length, axis=dim)
        initial = lax.slice_in_dim(shard, 0, width, axis=dim)
        before = lax.ppermute(last, axis, up)
        after = lax.ppermute(initial, axis, down)
        shard = jnp.concatenate([before, shard, after], axis=dim)
    return shard


def local_frame(values, blocks, axis):
    whole = (26 * blocks + 5) // 10
    left = (5 * whole - 13 * blocks).astype(F32) / 5.0
    shape = [1, 1, 1]
    shape[axis] = -1
    near = values - whole.astype(F32).reshape(shape)
    return (near + left.reshape(shape)) / CELL - 0.5


VMEM = pl.BlockSpec(memory_space=pltpu.VMEM)
PARAMS = pltpu.CompilerParams(vmem_limit_bytes=48 * 1024 * 1024)
SIDES = (("slab", 0), (("cross", "sub"), 1))


def shards(positions, velocities, pair_i, pair_j, pair_count, block_fill, block_body):
    length, width = block_fill.shape
    count = (length + 2) * (width + 2)
    slot_ids = lax.broadcasted_iota(jnp.int32, (length, width, 128), 2)
    masses = (slot_ids < block_fill[:, :, None]).astype(F32)
    rows = lax.axis_index("slab") * length + jnp.arange(length, dtype=jnp.int32)
    columns = lax.axis_index(("cross", "sub")) * width + jnp.arange(width, dtype=jnp.int32)
    x = local_frame(positions[0], rows, 0)
    y = local_frame(positions[1], columns, 1)
    z = (positions[2] - 9.45) / CELL
    state = jnp.stack(
        [x, y, z, masses, velocities[0], velocities[1], velocities[2], masses], axis=2
    )
    table = padded(state, SIDES, 1).reshape(count, 8, 128)
    scale, added = shift_tables()
    features, density, pressure = pl.pallas_call(
        lambda *refs: density_kernel(length, width, *refs),
        out_shape=(
            jax.ShapeDtypeStruct((count, 128, FEAT), BF16),
            jax.ShapeDtypeStruct((length, width, 128), F32),
            jax.ShapeDtypeStruct((length, width, 128), F32),
        ),
        in_specs=[VMEM] * 3,
        out_specs=(VMEM,) * 3,
        compiler_params=PARAMS,
        name="density",
    )(table, scale, added)
    framed_pressure = padded(pressure, SIDES, 1)
    hydro = pl.pallas_call(
        lambda *refs: force_kernel(length, width, *refs),
        out_shape=jax.ShapeDtypeStruct((3, length, width, 128), F32),
        in_specs=[VMEM] * 5,
        out_specs=VMEM,
        scratch_shapes=[pltpu.VMEM((count, 32, 256), BF16)],
        compiler_params=PARAMS,
        name="force",
    )(table, features, framed_pressure, scale, added)
    down = jnp.array([0.0, 0.0, GRAVITY], F32)[:, None, None, None]
    accel = hydro - down * masses[None]
    block_sums = jnp.sum(hydro, axis=3)
    bodies = lax.broadcasted_iota(jnp.int32, (NBODY, length, width), 0)
    owned = (block_body[None] == bodies).astype(F32)
    partial_force = jnp.sum(block_sums[:, None] * owned[None], axis=(2, 3))
    totals = lax.psum(partial_force, ("slab", "cross", "sub"))
    slot_total = (
        128
        * length
        * lax.axis_size("slab")
        * width
        * lax.axis_size("cross")
        * lax.axis_size("sub")
    )
    return (density, accel, totals / math.sqrt(slot_total))


def solution(mesh):
    placed = (
        P(None, ("tank", "slab"), ("cross", "sub"), None),
        P(None, ("tank", "slab"), ("cross", "sub"), None),
        P(("tank", "slab"), ("cross", "sub"), None),
        P(("tank", "slab"), ("cross", "sub"), None),
        P(("tank", "slab"), ("cross", "sub")),
        P(("tank", "slab"), ("cross", "sub")),
        P(("tank", "slab"), ("cross", "sub")),
    )
    return jax.shard_map(
        shards,
        mesh=mesh,
        in_specs=placed,
        out_specs=(
            P(("tank", "slab"), ("cross", "sub"), None),
            P(None, ("tank", "slab"), ("cross", "sub"), None),
            P(None, "tank"),
        ),
        check_vma=False,
    )
```

time: 1040 us -> 237 us (0.23)
  blocking collectives: 428 us -> 34.6 us
  other arithmetic: 258 us -> 6.1 us
  waiting for transfers between devices: 203 us -> 7.72 us
  Pallas kernels: 0 us -> 161 us
  local copies, waits for them, and re-layouts: 61.4 us -> 4.65 us
  loops' own time: 40.8 us -> 0 us
  starting transfers between devices: 46.9 us -> 21 us
    psum x1, blocking collectives: 428 us -> 34.6 us  [shards(): totals = lax.psum(partial_force, ('slab', 'cross', 'sub'))]
    ppermute x4, waiting for transfers between devices: 203 us -> 4.52 us  [padded(): after = lax.ppermute(initial, axis, down)]
    reduce_sum x131 -> x2, other arithmetic: 169 us -> 0.88 us  [the longest x1 0.77 us: shards(): block_sums = jnp.sum(hydro, axis=3)]
    pallas_call x0 -> x2, Pallas kernels: none -> 161 us  [the longest x1 88.3 us: shards(): pl.pallas_call(lambda *refs: force_kernel(length, width, *refs), out_shap...]
    gather x104 -> x0, local copies, waits for them, and re-layouts: 58.8 us -> none  [the longest x52 29.4 us: fetch_tiles(): jnp.take(table, second_ids, axis=0)]
    scatter-add x52 -> x0, other arithmetic: 48.4 us -> none  [store_values(): return carried.at[target_ids].add(values)]
    another operation x2 -> x0, loops' own time: 40.8 us -> none  [tile_loop(): return lax.fori_loop(first_group, last_group, advance, initial)]
    ppermute x4, starting transfers between devices: 41.7 us -> 15.9 us  [padded(): before = lax.ppermute(last, axis, up)]
  transfers between devices with their start and end apart: 8 -> 8, of which waited for: 4 -> 5; matrix products, arithmetic and copies ran while one was open for 0% -> 0% of each run, Pallas kernels for 0% -> 0%
where the time goes in v1:
time: 237 us; the launch traced here: 236 us
  Pallas kernels  161 us (68%)
  blocking collectives  34.6 us (15%)
  starting transfers between devices  21 us (9%)
  waiting for transfers between devices  7.72 us (3%)
  other arithmetic  6.1 us (3%)
  local copies, waits for them, and re-layouts  4.65 us (2%)
    pallas_call x1, Pallas kernels, shards(): pl.pallas_call(lambda *refs: force_kernel(length, width, *refs), out_shap...  88.3 us
    pallas_call x1, Pallas kernels, shards(): pl.pallas_call(lambda *refs: density_kernel(length, width, *refs), out_sh...  72.7 us
    psum x1, blocking collectives, shards(): totals = lax.psum(partial_force, ('slab', 'cross', 'sub'))  34.6 us
    ppermute x4, starting transfers between devices, padded(): before = lax.ppermute(last, axis, up)  15.9 us
    ppermute x4, starting transfers between devices, padded(): after = lax.ppermute(initial, axis, down)  5.17 us
  transfers between devices with their start and end apart: 8, of which 5 were waited for; matrix products, arithmetic and copies ran while one was open for 0% of the time, Pallas kernels for 0%

profile of v1, /device:TPU:0, one launch (start us, length us, event | category | flops | bytes accessed | tf_op | source)
XLA Modules:
  0.0 236.0 jit_solution(1871088836092073563)
XLA Ops:
  0.6 0.0 copy-start.1
  0.6 0.0 copy-start.3
  0.7 0.0 copy-start.4
  0.8 0.9 fusion.7
  1.7 0.9 fusion.3
  2.6 0.9 bitcast_dynamic-update-slice_fusion.3
  3.5 0.8 convert_dynamic-update-slice_fusion
  4.3 0.8 bitcast_dynamic-update-slice_fusion.2
  5.1 0.8 bitcast_dynamic-update-slice_fusion.1
  6.0 0.8 bitcast_dynamic-update-slice_fusion
  6.8 0.8 convert_dynamic-update-slice_fusion.1
  7.6 1.3 collective-permute-start.1
  8.9 5.6 %collective-permute-start = (f32[1,16,8,128]{3,1,0,2:T(8,128)S(1)}, f32[1,16,8,128]{3,1,0,2:T(8,128)S(1)}, u32[]{:S(2)}, u32[]{:S(2)}) collective-permute-start(f32[1,16,8,128]{3,1,0,2:T(8,128)S(1)} %get-tuple-element.11), channel_id=1, source_target_pairs={{0,4},{4,8},{8,12},{1,5},{5,9},{9,13},{2,6},{6,10},{10,14},{3,7},{... | collective-permute-start | bytes 196616 | tf_op jit(solution)/shard_map/ppermute | solution.py:199
  14.5 0.3 collective-permute-done.1
  14.8 1.6 collective-permute-done
  16.3 0.1 pad_maximum_fusion.4
  16.4 1.3 collective-permute-start.3
  17.7 0.0 copy-start.5
  17.7 3.0 %collective-permute-start.2 = (f32[10,1,8,128]{3,1,0,2:T(1,128)S(1)}, f32[10,1,8,128]{3,1,0,2:T(1,128)S(1)}, u32[]{:S(2)}, u32[]{:S(2)}) collective-permute-start(f32[10,1,8,128]{3,1,0,2:T(1,128)S(1)} %get-tuple-element.9), channel_id=1, source_target_pairs={{0,1},{1,2},{2,3},{4,5},{5,6},{6,7},{8,9},{9,10},{10,11},{12,13},{... | collective-permute-start | bytes 122888 | tf_op jit(solution)/shard_map/ppermute | solution.py:199
  20.8 0.0 collective-permute-done.3
  20.8 0.8 collective-permute-done.2
  21.6 0.2 pad_maximum_fusion
  21.8 0.2 copy.11
  22.0 0.0 copy-start
  22.0 0.9 copy-done
  22.9 0.0 copy-start.2
  22.9 0.9 copy-done.2
  23.8 72.7 %density.1 = (bf16[180,128,64]{2,1,0:T(8,128)(2,1)}, f32[8,16,128]{2,1,0:T(8,128)}, f32[8,16,128]{2,1,0:T(8,128)S(1)}) custom-call(f32[180,8,128]{2,1,0:T(8,128)S(1)} %bitcast.29, bf16[9,64,128]{2,1,0:T(8,128)(2,1)S(1)} %copy-done, bf16[9,64,128]{2,1,0:T(8,128)(2,1)S(1)} %copy-done.2), custom_call_target="tpu_custom_call" | custom-call | tf_op jit(solution)/shard_map/density/pallas_call | solution.py:234
  96.5 4.3 %collective-permute-start.4 = (f32[1,16,128]{2,1,0:T(8,128)S(1)}, f32[1,16,128]{2,1,0:T(8,128)S(1)}, u32[]{:S(2)}, u32[]{:S(2)}) collective-permute-start(f32[1,16,128]{2,1,0:T(8,128)S(1)} %get-tuple-element.18), channel_id=1, source_target_pairs={{0,4},{4,8},{8,12},{1,5},{5,9},{9,13},{2,6},{6,10},{10,14},{3,7},{... | collective-permute-start | bytes 24584 | tf_op jit(solution)/shard_map/ppermute | solution.py:199
  100.8 0.0 copy-done.3
  100.8 0.1 fusion.8
  100.9 1.3 collective-permute-start.5
  102.2 0.0 collective-permute-done.4
  102.2 4.2 %collective-permute-done.5 = f32[1,16,128]{2,1,0:T(8,128)S(1)} collective-permute-done((f32[1,16,128]{2,1,0:T(8,128)S(1)}, f32[1,16,128]{2,1,0:T(8,128)S(1)}, u32[]{:S(2)}, u32[]{:S(2)}) %collective-permute-start.5) | collective-permute-done | bytes 8224 | tf_op jit(solution)/shard_map/ppermute | solution.py:200
  106.4 1.3 collective-permute-start.7
  107.7 3.0 %collective-permute-start.6 = (f32[10,1,128]{2,1,0:T(1,128)S(1)}, f32[10,1,128]{2,1,0:T(1,128)S(1)}, u32[]{:S(2)}, u32[]{:S(2)}) collective-permute-start(f32[10,1,128]{2,1,0:T(1,128)S(1)} %get-tuple-element.15), channel_id=1, source_target_pairs={{0,1},{1,2},{2,3},{4,5},{5,6},{6,7},{8,9},{9,10},{10,11},{12,13},{... | collective-permute-start | bytes 15368 | tf_op jit(solution)/shard_map/ppermute | solution.py:199
  110.8 0.0 copy-done.4
  110.8 0.0 collective-permute-done.7
  110.8 0.8 collective-permute-done.6
  111.6 0.0 copy-done.1
  111.6 88.3 %force.1 = f32[3,8,16,128]{3,2,1,0:T(8,128)S(1)} custom-call(f32[180,8,128]{2,1,0:T(8,128)S(1)} %bitcast.30, bf16[180,128,64]{2,1,0:T(8,128)(2,1)} %get-tuple-element.7.refs_1_, f32[10,18,128]{2,1,0:T(8,128)S(1)} %pad_maximum_fusion.1.refs_2_, bf16[9,64,128]{2,1,0:T(8,128)(2,1)S(1)} %copy-done.1, bf16[9,64,128]{2,1,0:T(8,128)(2,1)S(1)} %copy-done.2), custom_call_target="tpu_custom_call" | custom-call | tf_op jit(solution)/shard_map/force/pallas_call | solution.py:247
  200.0 0.0 copy-done.5
  200.0 0.8 fusion.13
  200.7 0.1 multiply_reduce_fusion
  200.9 34.6 %psum.7 = f32[3,4]{1,0:T(4,128)S(1)} all-reduce(f32[3,4]{1,0:T(4,128)S(1)} %multiply_reduce_fusion), channel_id=1, replica_groups=mesh['tank'=2,'slab'=4,'cross'=2,'sub'=2] {'slab','cross','sub'}, use_global_device_ids=true, to_apply=%region_2.3 | all-reduce | flops 12 | bytes 96 | tf_op jit(solution)/shard_map/psum | solution.py:262
  235.5 0.6 broadcast_multiply_fusion
  (12 shorter events, 0.1 us)
Async XLA Ops:
  0.6 111.0 %copy-start.1 = (bf16[9,64,128]{2,1,0:T(8,128)(2,1)S(1)}, bf16[9,64,128]{2,1,0:T(8,128)(2,1)}, u32[]{:S(2)}) copy-start(bf16[9,64,128]{2,1,0:T(8,128)(2,1)} %constant.70.clone.refs_1_.refs_3_) | copy-start | bytes 442372
  0.6 100.1 %copy-start.3 = (s32[8,16]{1,0:T(8,128)S(1)}, s32[8,16]{1,0:T(8,128)}, u32[]{:S(2)}) copy-start(s32[8,16]{1,0:T(8,128)} %param.12) | copy-start | bytes 1540
  0.7 110.1 %copy-start.4 = (s32[8,16]{1,0:T(8,128)S(1)}, s32[8,16]{1,0:T(8,128)}, u32[]{:S(2)}) copy-start(s32[8,16]{1,0:T(8,128)} %param.13) | copy-start | bytes 1540
  7.6 7.2 %collective-permute-start.1 = (f32[1,16,8,128]{3,1,0,2:T(8,128)S(1)}, f32[1,16,8,128]{3,1,0,2:T(8,128)S(1)}, u32[]{:S(2)}, u32[]{:S(2)}) collective-permute-start(f32[1,16,8,128]{3,1,0,2:T(8,128)S(1)} %get-tuple-element.12), channel_id=1, source_target_pairs={{4,0},{8,4},{12,8},{5,1},{9,5},{13,9},{6,2},{10,6},{14,10},{7,3},{... | collective-permute-start | bytes 196616 | tf_op jit(solution)/shard_map/ppermute | solution.py:200
  8.9 7.5 %collective-permute-start = (f32[1,16,8,128]{3,1,0,2:T(8,128)S(1)}, f32[1,16,8,128]{3,1,0,2:T(8,128)S(1)}, u32[]{:S(2)}, u32[]{:S(2)}) collective-permute-start(f32[1,16,8,128]{3,1,0,2:T(8,128)S(1)} %get-tuple-element.11), channel_id=1, source_target_pairs={{0,4},{4,8},{8,12},{1,5},{5,9},{9,13},{2,6},{6,10},{10,14},{3,7},{... | collective-permute-start | bytes 196616 | tf_op jit(solution)/shard_map/ppermute | solution.py:199
  16.4 4.4 %collective-permute-start.3 = (f32[10,1,8,128]{3,1,0,2:T(1,128)S(1)}, f32[10,1,8,128]{3,1,0,2:T(1,128)S(1)}, u32[]{:S(2)}, u32[]{:S(2)}) collective-permute-start(f32[10,1,8,128]{3,1,0,2:T(1,128)S(1)} %get-tuple-element.10), channel_id=1, source_target_pairs={{1,0},{2,1},{3,2},{5,4},{6,5},{7,6},{9,8},{10,9},{11,10},{13,12},{... | collective-permute-start | bytes 122888 | tf_op jit(solution)/shard_map/ppermute | solution.py:200
  17.7 182.3 %copy-start.5 = (f32[3]{0:T(128)S(1)}, f32[3]{0:T(128)}, u32[]{:S(2)}) copy-start(f32[3]{0:T(128)} %constant.72.clone) | copy-start | bytes 40
  17.7 3.9 %collective-permute-start.2 = (f32[10,1,8,128]{3,1,0,2:T(1,128)S(1)}, f32[10,1,8,128]{3,1,0,2:T(1,128)S(1)}, u32[]{:S(2)}, u32[]{:S(2)}) collective-permute-start(f32[10,1,8,128]{3,1,0,2:T(1,128)S(1)} %get-tuple-element.9), channel_id=1, source_target_pairs={{0,1},{1,2},{2,3},{4,5},{5,6},{6,7},{8,9},{9,10},{10,11},{12,13},{... | collective-permute-start | bytes 122888 | tf_op jit(solution)/shard_map/ppermute | solution.py:199
  22.0 0.9 copy-start
  22.9 0.9 copy-start.2
  96.5 5.7 %collective-permute-start.4 = (f32[1,16,128]{2,1,0:T(8,128)S(1)}, f32[1,16,128]{2,1,0:T(8,128)S(1)}, u32[]{:S(2)}, u32[]{:S(2)}) collective-permute-start(f32[1,16,128]{2,1,0:T(8,128)S(1)} %get-tuple-element.18), channel_id=1, source_target_pairs={{0,4},{4,8},{8,12},{1,5},{5,9},{9,13},{2,6},{6,10},{10,14},{3,7},{... | collective-permute-start | bytes 24584 | tf_op jit(solution)/shard_map/ppermute | solution.py:199
  100.9 5.5 %collective-permute-start.5 = (f32[1,16,128]{2,1,0:T(8,128)S(1)}, f32[1,16,128]{2,1,0:T(8,128)S(1)}, u32[]{:S(2)}, u32[]{:S(2)}) collective-permute-start(f32[1,16,128]{2,1,0:T(8,128)S(1)} %get-tuple-element.17), channel_id=1, source_target_pairs={{4,0},{8,4},{12,8},{5,1},{9,5},{13,9},{6,2},{10,6},{14,10},{7,3},{... | collective-permute-start | bytes 24584 | tf_op jit(solution)/shard_map/ppermute | solution.py:200
  106.4 4.4 %collective-permute-start.7 = (f32[10,1,128]{2,1,0:T(1,128)S(1)}, f32[10,1,128]{2,1,0:T(1,128)S(1)}, u32[]{:S(2)}, u32[]{:S(2)}) collective-permute-start(f32[10,1,128]{2,1,0:T(1,128)S(1)} %get-tuple-element.16), channel_id=1, source_target_pairs={{1,0},{2,1},{3,2},{5,4},{6,5},{7,6},{9,8},{10,9},{11,10},{13,12},{... | collective-permute-start | bytes 15368 | tf_op jit(solution)/shard_map/ppermute | solution.py:200
  107.7 3.8 %collective-permute-start.6 = (f32[10,1,128]{2,1,0:T(1,128)S(1)}, f32[10,1,128]{2,1,0:T(1,128)S(1)}, u32[]{:S(2)}, u32[]{:S(2)}) collective-permute-start(f32[10,1,128]{2,1,0:T(1,128)S(1)} %get-tuple-element.15), channel_id=1, source_target_pairs={{0,1},{1,2},{2,3},{4,5},{5,6},{6,7},{8,9},{9,10},{10,11},{12,13},{... | collective-permute-start | bytes 15368 | tf_op jit(solution)/shard_map/ppermute | solution.py:199

commit v2 on v1

v2 whole, which is shorter than its diff:
```python
import math

import jax
import jax.numpy as jnp
import numpy as np
from jax import lax
from jax.experimental import pallas as pl
from jax.experimental.pallas import tpu as pltpu
from jax.sharding import PartitionSpec as P

NBODY = 4
SMOOTH = 1.3
CELL = 2.6
KERNEL_NORM = 21.0 / (16.0 * math.pi * SMOOTH**3)
SLOPE_NORM = 5.0 * KERNEL_NORM / SMOOTH**2
VISCOSITY = 0.2
GRAVITY = 1.0
FAR = 64.0
TINY = 1e-12
STEPS = [(da, db) for da in (-1, 0, 1) for db in (-1, 0, 1)]
FEAT = 64
F32, BF16 = jnp.float32, jnp.bfloat16


def shift_tables():
    scale = np.zeros((9, 8, 8, 128), np.float32)
    added = np.zeros((9, 8, 8, 128), np.float32)
    for k, (da, db) in enumerate(STEPS):
        scale[k, 0:6, 0:4] = 1.0
        scale[k, 0:3, 4] = 1.0
        scale[k, 0:3, 7] = -2.0 * da
        scale[k, 6, 4] = scale[k, 6, 7] = scale[k, 7, 4] = -2.0 * db
        for g in (0, 3, 5):
            added[k, g, 5] = 2.0 * da
            added[k, g, 6] = 2.0 * db
        added[k, 7, 7] = da * da + db * db
    return (
        jnp.asarray(scale.reshape(9, FEAT, 128), BF16),
        jnp.asarray(added.reshape(9, FEAT, 128), BF16),
    )


def split3(value):
    high = value.astype(BF16).astype(F32)
    rest = value - high
    middle = rest.astype(BF16).astype(F32)
    return high, middle, rest - middle


def norm_row(block):
    square = block * block
    return square[0:1] + square[1:2] + square[2:3]


def second_features(block):
    mass = block[3:4]
    x, y, z = block[0:1] * mass, block[1:2] * mass, block[2:3] * mass
    norm = jnp.where(mass > 0, norm_row(block), FAR)
    one = jnp.ones_like(mass)
    high, middle, low = split3(jnp.concatenate([x, y, z, norm, one, x, y, one], axis=0))
    rows = jnp.concatenate([high, high, high, middle, middle, low, high, high], axis=0)
    return rows.T.astype(BF16)


def first_features(block):
    x, y, z = block[0:1], block[1:2], block[2:3]
    zero = jnp.zeros_like(x)
    norm = norm_row(block)
    high, middle, low = split3(
        jnp.concatenate([-2.0 * x, -2.0 * y, -2.0 * z, zero, norm, y, zero, x], axis=0)
    )
    row = lax.broadcasted_iota(jnp.int32, (8, 128), 0)
    unit = (row == 3).astype(F32)
    g0, g1, g2 = high + unit, middle, low
    g6 = jnp.concatenate(
        [zero, zero, zero, zero, high[5:6], zero, zero, middle[5:6]], axis=0
    )
    g7 = jnp.concatenate([zero, zero, zero, zero, low[5:6], zero, zero, zero], axis=0)
    return jnp.concatenate([g0, g1, g2, g0, g1, g0, g6, g7], axis=0).astype(BF16)


def group_of(count):
    return next(n for n in (6, 5, 4, 3, 2, 1) if count % n == 0)


def pipelined(count, dots, process, first_buffer, second_buffer):
    dots(0, first_buffer)

    def step(pair, carry):
        dots(2 * pair + 1, second_buffer)
        process(2 * pair, first_buffer)
        dots(jnp.minimum(2 * pair + 2, count - 1), first_buffer)
        process(2 * pair + 1, second_buffer)
        return carry

    lax.fori_loop(0, count // 2, step, 0)


def square_dots(width, e_ref, a_ref, scale_ref, added_ref):
    frame = width + 2

    def dots(i, buffer):
        centre = (i // width + 1) * frame + i % width + 1
        base = first_features(e_ref[centre])
        for k, (da, db) in enumerate(STEPS):
            buffer[k] = jnp.dot(
                a_ref[centre + da * frame + db],
                base * scale_ref[k] + added_ref[k],
                preferred_element_type=F32,
            )

    return dots


def closeness(square):
    square = jnp.maximum(square, TINY)
    return jnp.maximum(1.0 - square * lax.rsqrt(square), 0.0)


def density_kernel(
    length, width, e_ref, scale_ref, added_ref, a_ref, dens_ref, table_ref, s0, s1
):
    frame = width + 2
    count = (length + 2) * frame
    group = group_of(count)

    def prepare(step, carry):
        made = [second_features(e_ref[step * group + n]) for n in range(group)]
        for n in range(group):
            a_ref[step * group + n] = made[n]
        return carry

    lax.fori_loop(0, count // group, prepare, 0)

    def process(i, buffer):
        row, column = i // width, i % width
        block = e_ref[(row + 1) * frame + column + 1]
        total = jnp.zeros((8, 128), F32)
        for k in range(9):
            rest = closeness(buffer[k])
            twice = rest * rest
            value = twice * twice * (1.25 - rest)
            total = total + jnp.sum(value.reshape(16, 8, 128), axis=0)
        mass = block[3:4]
        raw = (4.0 * KERNEL_NORM) * jnp.sum(total, axis=0, keepdims=True)
        dens_ref[row, pl.ds(column, 1), :] = raw * mass
        safe = jnp.where(mass > 0, raw, 1.0)
        square = safe * safe
        seventh = square * square * square * safe
        pressure = mass * (seventh - 1.0) / square
        place = lax.broadcasted_iota(jnp.int32, (8, 128), 0)
        table_ref[row, column] = jnp.where(place == 7, pressure, block)

    dots = square_dots(width, e_ref, a_ref, scale_ref, added_ref)
    pipelined(length * width, dots, process, s0, s1)


def force_kernel(
    length,
    width,
    body_ref,
    e_ref,
    a_ref,
    scale_ref,
    added_ref,
    accel_ref,
    sum_ref,
    c_ref,
    s0,
    s1,
):
    frame = width + 2
    count = (length + 2) * frame
    group = group_of(count)
    sum_ref[...] = jnp.zeros_like(sum_ref)

    def placed(block, row, column):
        lane = lax.broadcasted_iota(jnp.int32, (1, 128), 1)
        along = jnp.zeros_like(lane) + (row - length // 2)
        across = jnp.zeros_like(lane) + (column - width // 2)
        return (
            block[0:1] + along.astype(F32),
            block[1:2] + across.astype(F32),
            block[2:3],
        )

    def weights(e):
        block = e_ref[e]
        mass, pressure = block[3:4], block[7:8]
        spots = placed(block, e // frame - 1, e % frame - 1)
        rows = [mass, pressure] + [spot * mass for spot in spots]
        for d in range(3):
            rows.append(
                mass * (VISCOSITY * block[4 + d : 5 + d] - CELL * pressure * spots[d])
            )
        high, middle, low = split3(jnp.concatenate(rows, axis=0))
        part = jnp.concatenate(
            [high, middle, low, jnp.zeros_like(low)], axis=0
        ).astype(BF16)
        return jnp.concatenate([part, part], axis=1)

    def prepare(step, carry):
        made = [weights(step * group + n) for n in range(group)]
        for n in range(group):
            c_ref[step * group + n] = made[n]
        return carry

    lax.fori_loop(0, count // group, prepare, 0)

    def process(i, buffer):
        row, column = i // width, i % width
        centre = (row + 1) * frame + column + 1
        block = e_ref[centre]
        total = jnp.zeros((32, 128), F32)
        for k, (da, db) in enumerate(STEPS):
            rest = closeness(buffer[k])
            slope = rest * rest * rest
            high = slope.astype(BF16)
            low = (slope - high.astype(F32)).astype(BF16)
            total = total + jnp.dot(
                c_ref[centre + da * frame + db],
                jnp.concatenate([high, low], axis=0),
                preferred_element_type=F32,
            )
        sums = total[0:8] + total[8:16] + total[16:24]
        mass, pressure = block[3:4], block[7:8]
        spots = placed(block, row, column)
        rows = []
        for d in range(3):
            own = CELL * pressure * spots[d] - VISCOSITY * block[4 + d : 5 + d]
            value = (
                own * sums[0:1]
                + CELL * (spots[d] * sums[1:2] - pressure * sums[2 + d : 3 + d])
                + sums[5 + d : 6 + d]
            )
            hydro = SLOPE_NORM * mass * value
            rows.append(hydro)
            shown = hydro - GRAVITY * mass if d == 2 else hydro
            accel_ref[d, row, pl.ds(column, 1), :] = shown
        owner = body_ref[row, column]
        rows += [jnp.zeros((5, 128), F32)]
        sum_ref[owner] = sum_ref[owner] + jnp.concatenate(rows, axis=0)

    dots = square_dots(width, e_ref, a_ref, scale_ref, added_ref)
    pipelined(length * width, dots, process, s0, s1)


def sides():
    subs = lax.axis_size("sub")
    slab = lax.axis_index("slab")
    across = lax.axis_index("cross") * subs + lax.axis_index("sub")
    return slab, lax.axis_size("slab"), across, lax.axis_size("cross") * subs


def neighbour(slab, across):
    subs = lax.axis_size("sub")
    return {"slab": slab, "cross": across // subs, "sub": across % subs}


def halo(length, width, out_ref, send_sems, recv_sems):
    slab, slabs, across, acrosses = sides()
    away = [(da, db) for da, db in STEPS if (da, db) != (0, 0)]

    def inside(da, db):
        row, column = slab + da, across + db
        return (row >= 0) & (row < slabs) & (column >= 0) & (column < acrosses)

    barrier = pltpu.get_barrier_semaphore()
    near = jnp.int32(0)
    for da, db in away:

        @pl.when(inside(da, db))
        def _():
            pl.semaphore_signal(
                barrier, inc=1, device_id=neighbour(slab + da, across + db)
            )

        near = near + inside(da, db).astype(jnp.int32)
    pl.semaphore_wait(barrier, near)

    def edge(step, size):
        mine = {-1: (1, 1), 0: (1, size), 1: (size, 1)}[step]
        theirs = {-1: (size + 1, 1), 0: (1, size), 1: (0, 1)}[step]
        return pl.ds(*mine), pl.ds(*theirs)

    def copy(n, da, db, to_row, to_column):
        (from_a, to_a), (from_b, to_b) = edge(da, length), edge(db, width)
        return pltpu.make_async_remote_copy(
            src_ref=out_ref.at[from_a, from_b],
            dst_ref=out_ref.at[to_a, to_b],
            send_sem=send_sems.at[n],
            recv_sem=recv_sems.at[n],
            device_id=neighbour(to_row, to_column),
        )

    for n, (da, db) in enumerate(away):

        @pl.when(inside(da, db))
        def _():
            copy(n, da, db, slab + da, across + db).start()

    for n, (da, db) in enumerate(away):

        @pl.when(inside(da, db))
        def _():
            copy(n, da, db, slab + da, across + db).wait_send()

        @pl.when(inside(-da, -db))
        def _():
            copy(n, da, db, slab - da, across - db).wait_recv()


def clear_frame(length, width, out_ref):
    out_ref[0] = jnp.zeros(out_ref.shape[1:], F32)
    out_ref[length + 1] = jnp.zeros(out_ref.shape[1:], F32)

    def clear(row, carry):
        out_ref[row, 0] = jnp.zeros((8, 128), F32)
        out_ref[row, width + 1] = jnp.zeros((8, 128), F32)
        return carry

    lax.fori_loop(1, length + 1, clear, 0)


def pack_kernel(length, width, x_ref, v_ref, mass_ref, out_ref, send_sems, recv_sems):
    slab, _, across, _ = sides()
    clear_frame(length, width, out_ref)

    def frame_of(block):
        whole = (26 * block + 5) // 10
        return whole.astype(F32), (5 * whole - 13 * block).astype(F32) / 5.0

    def pack(row, carry):
        start_a, left_a = frame_of(slab * length + row)
        for column in range(width):
            start_b, left_b = frame_of(across * width + column)
            x = [x_ref[d, row, column : column + 1, :] for d in range(3)]
            v = [v_ref[d, row, column : column + 1, :] for d in range(3)]
            mass = mass_ref[row, column : column + 1, :]
            rows = [
                ((x[0] - start_a) + left_a) / CELL - 0.5,
                ((x[1] - start_b) + left_b) / CELL - 0.5,
                (x[2] - 9.45) / CELL,
                mass,
            ]
            out_ref[row + 1, column + 1] = jnp.concatenate(rows + v + [mass], axis=0)
        return carry

    lax.fori_loop(0, length, pack, 0)
    halo(length, width, out_ref, send_sems, recv_sems)


def frame_kernel(length, width, table_ref, out_ref, send_sems, recv_sems):
    clear_frame(length, width, out_ref)

    def place(row, carry):
        out_ref[row + 1, 1 : width + 1] = table_ref[row]
        return carry

    lax.fori_loop(0, length, place, 0)
    halo(length, width, out_ref, send_sems, recv_sems)


def total_kernel(part_ref, out_ref, held, near, far, send_sems, recv_sems):
    slab, slabs, across, acrosses = sides()
    barrier = pltpu.get_barrier_semaphore()
    beside = lambda n: neighbour(slab, lax.rem(across + n, acrosses))
    along = lambda n: neighbour(lax.rem(slab + n, slabs), across)
    for n in range(1, acrosses):
        pl.semaphore_signal(barrier, inc=1, device_id=beside(n))
    for n in range(1, slabs):
        pl.semaphore_signal(barrier, inc=1, device_id=along(n))
    pl.semaphore_wait(barrier, acrosses + slabs - 2)

    def swap(source, landing, size, peer, first):
        copies = []
        for n in range(1, size):
            copies.append(
                pltpu.make_async_remote_copy(
                    src_ref=source,
                    dst_ref=landing.at[n - 1],
                    send_sem=send_sems.at[first + n - 1],
                    recv_sem=recv_sems.at[first + n - 1],
                    device_id=peer(n),
                )
            )
            copies[-1].start()
        value = source[...]
        for n, copy in enumerate(copies):
            copy.wait()
            value = value + landing[n]
        return value

    held[...] = swap(part_ref, near, acrosses, beside, 0)
    value = swap(held, far, slabs, along, acrosses - 1)
    out_ref[...] = jnp.broadcast_to(jnp.sum(value, axis=2, keepdims=True), value.shape)


VMEM = pl.BlockSpec(memory_space=pltpu.VMEM)
SMEM = pl.BlockSpec(memory_space=pltpu.SMEM)
LIMIT = 48 * 1024 * 1024
PARAMS = pltpu.CompilerParams(vmem_limit_bytes=LIMIT)


def remote(number):
    return pltpu.CompilerParams(
        vmem_limit_bytes=LIMIT, collective_id=number, has_side_effects=True
    )


def shards(positions, velocities, pair_i, pair_j, pair_count, block_fill, block_body):
    length, width = block_fill.shape
    count = (length + 2) * (width + 2)
    slot_ids = lax.broadcasted_iota(jnp.int32, (length, width, 128), 2)
    masses = (slot_ids < block_fill[:, :, None]).astype(F32)
    framed = jax.ShapeDtypeStruct((length + 2, width + 2, 8, 128), F32)
    eight = [pltpu.SemaphoreType.DMA((8,))] * 2
    ahead = [pltpu.VMEM((9, 128, 128), F32)] * 2
    table = pl.pallas_call(
        lambda *refs: pack_kernel(length, width, *refs),
        out_shape=framed,
        in_specs=[VMEM] * 3,
        out_specs=VMEM,
        scratch_shapes=eight,
        compiler_params=remote(0),
        name="pack",
    )(positions, velocities, masses)
    scale, added = shift_tables()
    features, density, pressed = pl.pallas_call(
        lambda *refs: density_kernel(length, width, *refs),
        out_shape=(
            jax.ShapeDtypeStruct((count, 128, FEAT), BF16),
            jax.ShapeDtypeStruct((length, width, 128), F32),
            jax.ShapeDtypeStruct((length, width, 8, 128), F32),
        ),
        in_specs=[VMEM] * 3,
        out_specs=(VMEM,) * 3,
        scratch_shapes=ahead,
        compiler_params=PARAMS,
        name="density",
    )(table.reshape(count, 8, 128), scale, added)
    table = pl.pallas_call(
        lambda *refs: frame_kernel(length, width, *refs),
        out_shape=framed,
        in_specs=[VMEM],
        out_specs=VMEM,
        scratch_shapes=eight,
        compiler_params=remote(1),
        name="frame",
    )(pressed)
    accel, partial_force = pl.pallas_call(
        lambda *refs: force_kernel(length, width, *refs),
        out_shape=(
            jax.ShapeDtypeStruct((3, length, width, 128), F32),
            jax.ShapeDtypeStruct((NBODY + 1, 8, 128), F32),
        ),
        in_specs=[SMEM] + [VMEM] * 4,
        out_specs=(VMEM, VMEM),
        scratch_shapes=[pltpu.VMEM((count, 32, 256), BF16)] + ahead,
        compiler_params=PARAMS,
        name="force",
    )(block_body, table.reshape(count, 8, 128), features, scale, added)
    slabs = lax.axis_size("slab")
    acrosses = lax.axis_size("cross") * lax.axis_size("sub")
    one = partial_force.shape
    totals = pl.pallas_call(
        total_kernel,
        out_shape=jax.ShapeDtypeStruct(one, F32),
        in_specs=[VMEM],
        out_specs=VMEM,
        scratch_shapes=[
            pltpu.VMEM(one, F32),
            pltpu.VMEM((acrosses - 1,) + one, F32),
            pltpu.VMEM((slabs - 1,) + one, F32),
        ]
        + [pltpu.SemaphoreType.DMA((acrosses + slabs - 2,))] * 2,
        compiler_params=remote(2),
        name="total",
    )(partial_force)
    slot_total = 128 * length * slabs * width * acrosses
    body_force = totals[:NBODY, :3, 0].T / math.sqrt(slot_total)
    return (density, accel, body_force)


def solution(mesh):
    placed = (
        P(None, ("tank", "slab"), ("cross", "sub"), None),
        P(None, ("tank", "slab"), ("cross", "sub"), None),
        P(("tank", "slab"), ("cross", "sub"), None),
        P(("tank", "slab"), ("cross", "sub"), None),
        P(("tank", "slab"), ("cross", "sub")),
        P(("tank", "slab"), ("cross", "sub")),
        P(("tank", "slab"), ("cross", "sub")),
    )
    return jax.shard_map(
        shards,
        mesh=mesh,
        in_specs=placed,
        out_specs=(
            P(("tank", "slab"), ("cross", "sub"), None),
            P(None, ("tank", "slab"), ("cross", "sub"), None),
            P(None, "tank"),
        ),
        check_vma=False,
    )
```

time: 237 us -> 131 us (0.55)
  Pallas kernels: 161 us -> 123 us
  blocking collectives: 34.6 us -> 0 us
  starting transfers between devices: 21 us -> 0 us
  waiting for transfers between devices: 7.72 us -> 0 us
  other arithmetic: 6.1 us -> 0.85 us
    psum x1 -> x0, blocking collectives: 34.6 us -> none  [shards(): totals = lax.psum(partial_force, ('slab', 'cross', 'sub'))]
    pallas_call x1, Pallas kernels: 88.3 us -> 53.8 us  [shards(): pl.pallas_call(lambda *refs: force_kernel(length, width, *refs), out_shap...]
    pallas_call x1, Pallas kernels: 72.7 us -> 46.1 us  [shards(): pl.pallas_call(lambda *refs: density_kernel(length, width, *refs), out_sh...]
    pallas_call x0 -> x3, Pallas kernels: none -> 23.3 us  [the longest x1 9.87 us: shards(): pl.pallas_call(total_kernel, out_shape=jax.ShapeDtypeStruct(one, F32), in...]
    ppermute x8 -> x0, starting transfers between devices: 21 us -> none  [the longest x4 15.9 us: padded(): before = lax.ppermute(last, axis, up)]
    ppermute x8 -> x0, waiting for transfers between devices: 7.72 us -> none  [the longest x4 4.52 us: padded(): after = lax.ppermute(initial, axis, down)]
    unnamed x4 -> x0, other arithmetic: 3.47 us -> none
    unnamed x17 -> x13, local copies, waits for them, and re-layouts: 4.38 us -> 5.92 us
  transfers between devices with their start and end apart: 8 -> 0, of which waited for: 5 -> 0; matrix products, arithmetic and copies ran while one was open for 0% -> 0% of each run, Pallas kernels for 0% -> 0%
where the time goes in v2:
time: 131 us
  Pallas kernels  123 us (94%)
  local copies, waits for them, and re-layouts  5.92 us (5%)
    pallas_call x1, Pallas kernels, shards(): pl.pallas_call(lambda *refs: force_kernel(length, width, *refs), out_shap...  53.8 us
    pallas_call x1, Pallas kernels, shards(): pl.pallas_call(lambda *refs: density_kernel(length, width, *refs), out_sh...  46.1 us
    pallas_call x1, Pallas kernels, shards(): pl.pallas_call(total_kernel, out_shape=jax.ShapeDtypeStruct(one, F32), in...  9.87 us
    pallas_call x1, Pallas kernels, shards(): pl.pallas_call(lambda *refs: pack_kernel(length, width, *refs), out_shape...  8.61 us
    unnamed x13, local copies, waits for them, and re-layouts  5.92 us
    pallas_call x1, Pallas kernels, shards(): pl.pallas_call(lambda *refs: frame_kernel(length, width, *refs), out_shap...  4.81 us

profile of v2, /device:TPU:0, one launch (start us, length us, event | category | flops | bytes accessed | tf_op | source)
XLA Modules:
  0.0 130.6 jit_solution(10117483518746792636)
XLA Ops:
  0.6 0.8 fusion.refs_2_
  1.4 0.0 copy-start.3
  1.4 0.9 copy-done.3
  2.3 0.0 copy-start.4
  2.3 0.9 copy-done.4
  3.3 8.6 %pack.1 = f32[10,18,8,128]{3,2,1,0:T(8,128)S(1)} custom-call(f32[3,8,16,128]{3,2,1,0:T(8,128)S(1)} %copy-done.3, f32[3,8,16,128]{3,2,1,0:T(8,128)S(1)} %copy-done.4, f32[8,16,128]{2,1,0:T(8,128)S(1)} %fusion.refs_2_), custom_call_target="tpu_custom_call" | custom-call | tf_op jit(solution)/shard_map/pack/pallas_call | solution.py:419
  11.9 0.0 copy-start
  11.9 0.9 copy-done
  12.8 0.0 copy-start.1
  12.8 0.9 copy-done.1
  13.7 46.1 %density.1 = (bf16[180,128,64]{2,1,0:T(8,128)(2,1)}, f32[8,16,128]{2,1,0:T(8,128)}, f32[8,16,8,128]{3,2,1,0:T(8,128)S(1)}) custom-call(f32[180,8,128]{2,1,0:T(8,128)S(1)} %bitcast.4, bf16[9,64,128]{2,1,0:T(8,128)(2,1)S(1)} %copy-done.1, bf16[9,64,128]{2,1,0:T(8,128)(2,1)S(1)} %copy-done), custom_call_target="tpu_custom_call" | custom-call | tf_op jit(solution)/shard_map/density/pallas_call | solution.py:429
  59.8 4.8 %frame.1 = f32[10,18,8,128]{3,2,1,0:T(8,128)S(1)} custom-call(f32[8,16,8,128]{3,2,1,0:T(8,128)S(1)} %get-tuple-element.9.refs_0_), custom_call_target="tpu_custom_call" | custom-call | tf_op jit(solution)/shard_map/frame/pallas_call | solution.py:442
  64.6 0.0 copy-start.2
  64.6 0.9 copy-done.2
  65.5 0.0 copy-start.5
  65.5 0.7 copy-done.5
  66.2 53.8 %force.1 = (f32[3,8,16,128]{3,2,1,0:T(8,128)}, f32[5,8,128]{2,1,0:T(8,128)S(1)}) custom-call(s32[8,16]{1,0:T(8,128)S(1)} %copy-done.5, f32[180,8,128]{2,1,0:T(8,128)S(1)} %bitcast.3, bf16[180,128,64]{2,1,0:T(8,128)(2,1)} %get-tuple-element.10.refs_2_, bf16[9,64,128]{2,1,0:T(8,128)(2,1)S(1)} %copy-done.2, bf16[9,64,128]{2,1,0:T(8,128)(2,1)S(1)} %copy-done), custom_call_target="tpu_custom_call" | custom-call | tf_op jit(solution)/shard_map/force/pallas_call | solution.py:451
  120.0 9.9 %total.1 = f32[5,8,128]{2,1,0:T(8,128)S(1)} custom-call(f32[5,8,128]{2,1,0:T(8,128)S(1)} %get-tuple-element.12.part_ref), custom_call_target="tpu_custom_call" | custom-call | tf_op jit(solution)/shard_map/total/pallas_call | solution.py:466
  129.9 0.1 multiply_reduce_fusion
  130.0 0.7 copy.10
Async XLA Ops:
  1.4 0.9 copy-start.3
  2.3 0.9 copy-start.4
  11.9 0.9 copy-start
  12.8 0.9 copy-start.1
  64.6 0.9 copy-start.2
  65.5 0.7 copy-start.5

commit v3 on v2

--- a/solution.py
+++ b/solution.py
@@ -2,7 +2,6 @@
 
 import jax
 import jax.numpy as jnp
-import numpy as np
 from jax import lax
 from jax.experimental import pallas as pl
 from jax.experimental.pallas import tpu as pltpu
@@ -15,29 +14,18 @@
 SLOPE_NORM = 5.0 * KERNEL_NORM / SMOOTH**2
 VISCOSITY = 0.2
 GRAVITY = 1.0
-FAR = 64.0
+FAR = 1024.0
 TINY = 1e-12
 STEPS = [(da, db) for da in (-1, 0, 1) for db in (-1, 0, 1)]
-FEAT = 64
+FEAT = 48
 F32, BF16 = jnp.float32, jnp.bfloat16
 
 
-def shift_tables():
-    scale = np.zeros((9, 8, 8, 128), np.float32)
-    added = np.zeros((9, 8, 8, 128), np.float32)
-    for k, (da, db) in enumerate(STEPS):
-        scale[k, 0:6, 0:4] = 1.0
-        scale[k, 0:3, 4] = 1.0
-        scale[k, 0:3, 7] = -2.0 * da
-        scale[k, 6, 4] = scale[k, 6, 7] = scale[k, 7, 4] = -2.0 * db
-        for g in (0, 3, 5):
-            added[k, g, 5] = 2.0 * da
-            added[k, g, 6] = 2.0 * db
-        added[k, 7, 7] = da * da + db * db
-    return (
-        jnp.asarray(scale.reshape(9, FEAT, 128), BF16),
-        jnp.asarray(added.reshape(9, FEAT, 128), BF16),
-    )
+def placed(block, row, column, length, width):
+    lane = lax.broadcasted_iota(jnp.int32, (1, 128), 1)
+    along = (jnp.zeros_like(lane) + row).astype(F32) - 0.5 * (length - 1)
+    across = (jnp.zeros_like(lane) + column).astype(F32) - 0.5 * (width - 1)
+    return block[0:1] + along, block[1:2] + across, block[2:3]
 
 
 def split3(value):
@@ -47,36 +35,29 @@
     return high, middle, rest - middle
 
 
-def norm_row(block):
-    square = block * block
-    return square[0:1] + square[1:2] + square[2:3]
-
-
-def second_features(block):
-    mass = block[3:4]
-    x, y, z = block[0:1] * mass, block[1:2] * mass, block[2:3] * mass
-    norm = jnp.where(mass > 0, norm_row(block), FAR)
-    one = jnp.ones_like(mass)
-    high, middle, low = split3(jnp.concatenate([x, y, z, norm, one, x, y, one], axis=0))
-    rows = jnp.concatenate([high, high, high, middle, middle, low, high, high], axis=0)
-    return rows.T.astype(BF16)
-
-
-def first_features(block):
-    x, y, z = block[0:1], block[1:2], block[2:3]
+def second_features(spots, mass):
+    x, y, z = [spot * mass for spot in spots]
+    norm = jnp.where(mass > 0, x * x + y * y + z * z, FAR)
+    one, zero = jnp.ones_like(mass), jnp.zeros_like(mass)
+    high, middle, low = split3(
+        jnp.concatenate([x, y, z, norm, one, zero, zero, zero], axis=0)
+    )
+    rows = jnp.concatenate([high, high, high, middle, middle, low], axis=0)
+    return jnp.concatenate([rows, jnp.zeros((16, 128), F32)], axis=0).T[:, :FEAT].astype(BF16)
+
+
+def first_features(spots):
+    x, y, z = spots
     zero = jnp.zeros_like(x)
-    norm = norm_row(block)
+    norm = x * x + y * y + z * z
     high, middle, low = split3(
-        jnp.concatenate([-2.0 * x, -2.0 * y, -2.0 * z, zero, norm, y, zero, x], axis=0)
+        jnp.concatenate(
+            [-2.0 * x, -2.0 * y, -2.0 * z, zero, norm, zero, zero, zero], axis=0
+        )
     )
-    row = lax.broadcasted_iota(jnp.int32, (8, 128), 0)
-    unit = (row == 3).astype(F32)
-    g0, g1, g2 = high + unit, middle, low
-    g6 = jnp.concatenate(
-        [zero, zero, zero, zero, high[5:6], zero, zero, middle[5:6]], axis=0
-    )
-    g7 = jnp.concatenate([zero, zero, zero, zero, low[5:6], zero, zero, zero], axis=0)
-    return jnp.concatenate([g0, g1, g2, g0, g1, g0, g6, g7], axis=0).astype(BF16)
+    unit = (lax.broadcasted_iota(jnp.int32, (8, 128), 0) == 3).astype(F32)
+    high = high + unit
+    return jnp.concatenate([high, middle, low, high, middle, high], axis=0).astype(BF16)
 
 
 def group_of(count):
@@ -96,17 +77,16 @@
     lax.fori_loop(0, count // 2, step, 0)
 
 
-def square_dots(width, e_ref, a_ref, scale_ref, added_ref):
+def square_dots(length, width, e_ref, a_ref):
     frame = width + 2
 
     def dots(i, buffer):
-        centre = (i // width + 1) * frame + i % width + 1
-        base = first_features(e_ref[centre])
+        row, column = i // width, i % width
+        centre = (row + 1) * frame + column + 1
+        first = first_features(placed(e_ref[centre], row, column, length, width))
         for k, (da, db) in enumerate(STEPS):
             buffer[k] = jnp.dot(
-                a_ref[centre + da * frame + db],
-                base * scale_ref[k] + added_ref[k],
-                preferred_element_type=F32,
+                a_ref[centre + da * frame + db], first, preferred_element_type=F32
             )
 
     return dots
@@ -118,14 +98,19 @@
 
 
 def density_kernel(
-    length, width, e_ref, scale_ref, added_ref, a_ref, dens_ref, table_ref, s0, s1
+    length, width, e_ref, a_ref, dens_ref, table_ref, s0, s1
 ):
     frame = width + 2
     count = (length + 2) * frame
     group = group_of(count)
 
     def prepare(step, carry):
-        made = [second_features(e_ref[step * group + n]) for n in range(group)]
+        made = []
+        for n in range(group):
+            e = step * group + n
+            block = e_ref[e]
+            spots = placed(block, e // frame - 1, e % frame - 1, length, width)
+            made.append(second_features(spots, block[3:4]))
         for n in range(group):
             a_ref[step * group + n] = made[n]
         return carry
@@ -151,7 +136,7 @@
         place = lax.broadcasted_iota(jnp.int32, (8, 128), 0)
         table_ref[row, column] = jnp.where(place == 7, pressure, block)
 
-    dots = square_dots(width, e_ref, a_ref, scale_ref, added_ref)
+    dots = square_dots(length, width, e_ref, a_ref)
     pipelined(length * width, dots, process, s0, s1)
 
 
@@ -161,8 +146,6 @@
     body_ref,
     e_ref,
     a_ref,
-    scale_ref,
-    added_ref,
     accel_ref,
     sum_ref,
     c_ref,
@@ -174,20 +157,10 @@
     group = group_of(count)
     sum_ref[...] = jnp.zeros_like(sum_ref)
 
-    def placed(block, row, column):
-        lane = lax.broadcasted_iota(jnp.int32, (1, 128), 1)
-        along = jnp.zeros_like(lane) + (row - length // 2)
-        across = jnp.zeros_like(lane) + (column - width // 2)
-        return (
-            block[0:1] + along.astype(F32),
-            block[1:2] + across.astype(F32),
-            block[2:3],
-        )
-
     def weights(e):
         block = e_ref[e]
         mass, pressure = block[3:4], block[7:8]
-        spots = placed(block, e // frame - 1, e % frame - 1)
+        spots = placed(block, e // frame - 1, e % frame - 1, length, width)
         rows = [mass, pressure] + [spot * mass for spot in spots]
         for d in range(3):
             rows.append(
@@ -212,19 +185,29 @@
         centre = (row + 1) * frame + column + 1
         block = e_ref[centre]
         total = jnp.zeros((32, 128), F32)
-        for k, (da, db) in enumerate(STEPS):
+
+        def halves(k):
             rest = closeness(buffer[k])
             slope = rest * rest * rest
             high = slope.astype(BF16)
             low = (slope - high.astype(F32)).astype(BF16)
-            total = total + jnp.dot(
-                c_ref[centre + da * frame + db],
-                jnp.concatenate([high, low], axis=0),
+            return jnp.concatenate([high, low], axis=0)
+
+        def features(k):
+            da, db = STEPS[k]
+            return c_ref[centre + da * frame + db]
+
+        for k in range(0, 8, 2):
+            both = jnp.dot(
+                jnp.concatenate([features(k), features(k + 1)], axis=0),
+                jnp.concatenate([halves(k), halves(k + 1)], axis=1),
                 preferred_element_type=F32,
             )
+            total = total + both[0:32, 0:128] + both[32:64, 128:256]
+        total = total + jnp.dot(features(8), halves(8), preferred_element_type=F32)
         sums = total[0:8] + total[8:16] + total[16:24]
         mass, pressure = block[3:4], block[7:8]
-        spots = placed(block, row, column)
+        spots = placed(block, row, column, length, width)
         rows = []
         for d in range(3):
             own = CELL * pressure * spots[d] - VISCOSITY * block[4 + d : 5 + d]
@@ -241,7 +224,7 @@
         rows += [jnp.zeros((5, 128), F32)]
         sum_ref[owner] = sum_ref[owner] + jnp.concatenate(rows, axis=0)
 
-    dots = square_dots(width, e_ref, a_ref, scale_ref, added_ref)
+    dots = square_dots(length, width, e_ref, a_ref)
     pipelined(length * width, dots, process, s0, s1)
 
 
@@ -322,8 +305,9 @@
     lax.fori_loop(1, length + 1, clear, 0)
 
 
-def pack_kernel(length, width, x_ref, v_ref, mass_ref, out_ref, send_sems, recv_sems):
+def pack_kernel(length, width, x_ref, v_ref, fill_ref, out_ref, send_sems, recv_sems):
     slab, _, across, _ = sides()
+    slot = lax.broadcasted_iota(jnp.int32, (1, 128), 1)
     clear_frame(length, width, out_ref)
 
     def frame_of(block):
@@ -336,7 +320,7 @@
             start_b, left_b = frame_of(across * width + column)
             x = [x_ref[d, row, column : column + 1, :] for d in range(3)]
             v = [v_ref[d, row, column : column + 1, :] for d in range(3)]
-            mass = mass_ref[row, column : column + 1, :]
+            mass = (slot < fill_ref[row, column]).astype(F32)
             rows = [
                 ((x[0] - start_a) + left_a) / CELL - 0.5,
                 ((x[1] - start_b) + left_b) / CELL - 0.5,
@@ -411,21 +395,18 @@
 def shards(positions, velocities, pair_i, pair_j, pair_count, block_fill, block_body):
     length, width = block_fill.shape
     count = (length + 2) * (width + 2)
-    slot_ids = lax.broadcasted_iota(jnp.int32, (length, width, 128), 2)
-    masses = (slot_ids < block_fill[:, :, None]).astype(F32)
     framed = jax.ShapeDtypeStruct((length + 2, width + 2, 8, 128), F32)
     eight = [pltpu.SemaphoreType.DMA((8,))] * 2
     ahead = [pltpu.VMEM((9, 128, 128), F32)] * 2
     table = pl.pallas_call(
         lambda *refs: pack_kernel(length, width, *refs),
         out_shape=framed,
-        in_specs=[VMEM] * 3,
+        in_specs=[VMEM, VMEM, SMEM],
         out_specs=VMEM,
         scratch_shapes=eight,
         compiler_params=remote(0),
         name="pack",
-    )(positions, velocities, masses)
-    scale, added = shift_tables()
+    )(positions, velocities, block_fill)
     features, density, pressed = pl.pallas_call(
         lambda *refs: density_kernel(length, width, *refs),
         out_shape=(
@@ -433,12 +414,12 @@
             jax.ShapeDtypeStruct((length, width, 128), F32),
             jax.ShapeDtypeStruct((length, width, 8, 128), F32),
         ),
-        in_specs=[VMEM] * 3,
+        in_specs=[VMEM],
         out_specs=(VMEM,) * 3,
         scratch_shapes=ahead,
         compiler_params=PARAMS,
         name="density",
-    )(table.reshape(count, 8, 128), scale, added)
+    )(table.reshape(count, 8, 128))
     table = pl.pallas_call(
         lambda *refs: frame_kernel(length, width, *refs),
         out_shape=framed,
@@ -454,12 +435,12 @@
             jax.ShapeDtypeStruct((3, length, width, 128), F32),
             jax.ShapeDtypeStruct((NBODY + 1, 8, 128), F32),
         ),
-        in_specs=[SMEM] + [VMEM] * 4,
+        in_specs=[SMEM] + [VMEM] * 2,
         out_specs=(VMEM, VMEM),
         scratch_shapes=[pltpu.VMEM((count, 32, 256), BF16)] + ahead,
         compiler_params=PARAMS,
         name="force",
-    )(block_body, table.reshape(count, 8, 128), features, scale, added)
+    )(block_body, table.reshape(count, 8, 128), features)
     slabs = lax.axis_size("slab")
     acrosses = lax.axis_size("cross") * lax.axis_size("sub")
     one = partial_force.shape

time: 131 us -> 125 us (0.954)
  Pallas kernels: 123 us -> 120 us
  local copies, waits for them, and re-layouts: 5.92 us -> 3.88 us
    pallas_call x1, Pallas kernels: 53.8 us -> 49.6 us  [shards(): pl.pallas_call(lambda *refs: force_kernel(length, width, *refs), out_shap...]
    unnamed x13 -> x9, local copies, waits for them, and re-layouts: 5.92 us -> 3.88 us
where the time goes in v3:
time: 125 us; the launch traced here: 124 us
  Pallas kernels  120 us (96%)
  local copies, waits for them, and re-layouts  3.88 us (3%)
    pallas_call x1, Pallas kernels, shards(): pl.pallas_call(lambda *refs: force_kernel(length, width, *refs), out_shap...  49.6 us
    pallas_call x1, Pallas kernels, shards(): pl.pallas_call(lambda *refs: density_kernel(length, width, *refs), out_sh...  46.1 us
    pallas_call x1, Pallas kernels, shards(): pl.pallas_call(total_kernel, out_shape=jax.ShapeDtypeStruct(one, F32), in...  9.9 us
    pallas_call x1, Pallas kernels, shards(): pl.pallas_call(lambda *refs: pack_kernel(length, width, *refs), out_shape...  9.26 us
    pallas_call x1, Pallas kernels, shards(): pl.pallas_call(lambda *refs: frame_kernel(length, width, *refs), out_shap...  4.78 us
    unnamed x9, local copies, waits for them, and re-layouts  3.88 us

profile of v3, /device:TPU:0, one launch (start us, length us, event | category | flops | bytes accessed | tf_op | source)
XLA Modules:
  0.0 124.3 jit_solution(18053588225476925932)
XLA Ops:
  0.6 0.0 copy-start
  0.6 0.9 copy-done
  1.6 0.0 copy-start.1
  1.6 0.9 copy-done.1
  2.5 0.0 copy-start.2
  2.5 0.7 copy-done.2
  3.2 9.3 %pack.1 = f32[10,18,8,128]{3,2,1,0:T(8,128)S(1)} custom-call(f32[3,8,16,128]{3,2,1,0:T(8,128)S(1)} %copy-done, f32[3,8,16,128]{3,2,1,0:T(8,128)S(1)} %copy-done.1, s32[8,16]{1,0:T(8,128)S(1)} %copy-done.2), custom_call_target="tpu_custom_call" | custom-call | tf_op jit(solution)/shard_map/pack/pallas_call | solution.py:401
  12.4 46.1 %density.1 = (bf16[180,128,48]{2,1,0:T(8,128)(2,1)}, f32[8,16,128]{2,1,0:T(8,128)}, f32[8,16,8,128]{3,2,1,0:T(8,128)S(1)}) custom-call(f32[180,8,128]{2,1,0:T(8,128)S(1)} %bitcast.4), custom_call_target="tpu_custom_call" | custom-call | tf_op jit(solution)/shard_map/density/pallas_call | solution.py:410
  58.6 4.8 %frame.1 = f32[10,18,8,128]{3,2,1,0:T(8,128)S(1)} custom-call(f32[8,16,8,128]{3,2,1,0:T(8,128)S(1)} %get-tuple-element.9.refs_0_), custom_call_target="tpu_custom_call" | custom-call | tf_op jit(solution)/shard_map/frame/pallas_call | solution.py:423
  63.4 0.0 copy-start.3
  63.4 0.7 copy-done.3
  64.1 49.6 %force.1 = (f32[3,8,16,128]{3,2,1,0:T(8,128)}, f32[5,8,128]{2,1,0:T(8,128)S(1)}) custom-call(s32[8,16]{1,0:T(8,128)S(1)} %copy-done.3, f32[180,8,128]{2,1,0:T(8,128)S(1)} %bitcast.3, bf16[180,128,48]{2,1,0:T(8,128)(2,1)} %get-tuple-element.10.refs_2_), custom_call_target="tpu_custom_call" | custom-call | tf_op jit(solution)/shard_map/force/pallas_call | solution.py:432
  113.7 9.9 %total.1 = f32[5,8,128]{2,1,0:T(8,128)S(1)} custom-call(f32[5,8,128]{2,1,0:T(8,128)S(1)} %get-tuple-element.12.part_ref), custom_call_target="tpu_custom_call" | custom-call | tf_op jit(solution)/shard_map/total/pallas_call | solution.py:447
  123.6 0.1 multiply_reduce_fusion
  123.7 0.7 copy.8
Async XLA Ops:
  0.6 0.9 copy-start
  1.6 0.9 copy-start.1
  2.5 0.7 copy-start.2
  63.4 0.7 copy-start.3
